TPU v7x, 256 devices: a whole 4x4x8 slice. The times are simulated.
256 devices in a mesh: bl: 8 (over z), lst: 32 (over y, x, core).
Axes of the slice: x: 4, y: 4, z: 8, core: 2. Of those that a mesh axis runs over, the one named last changes fastest.
Arguments:
- visibility: bfloat16 [4, 1024, 32, 3072], P(None, 'lst', 'bl'), may hold values from -6 to 6
- start_bin: int32 [4], replicated, may hold values from 0 to 1023
- coverage: int32 [4], replicated, may hold values from 256 to 1024
- clip_flags: int32 [4, 1024, 32], P(None, 'lst', 'bl'), may hold values 0 or 1
- fringe_filter: bfloat16 [1024, 1024], P('bl'), may hold values from -0.1875 to 0.1875
Outputs:
- filtered: bfloat16 [1024, 32, 3072], P('lst', 'bl')
- spread: bfloat16 [1024, 32, 3072], P('lst', 'bl')
All inputs are finite; a program needn't handle non-finite values. No bound on the sum of `clip_flags` on one device may be relied on, other than what follows from the above.
Results may differ from a plain program's by a relative error of at most 0.0047.
Values may be sent and summed in bfloat16 or wider, within the bound.
A program may use at most 128 MiB of HBM per device.

v0:
```python
from functools import partial

import jax
import jax.numpy as jnp
from jax import lax
from jax.sharding import PartitionSpec as P


def from_behind(shard, axis, by):
    devices = lax.axis_size(axis)
    return lax.ppermute(shard, axis, [(i, (i + by) % devices) for i in range(devices)])


def slide_rows(series, first_row, length):
    return lax.dynamic_slice_in_dim(series, first_row, length, 0)


def statistic_moments(aligned, weight):
    values = aligned.astype(jnp.float32)
    weight_sum = jnp.sum(weight, axis=0)
    average = jnp.sum(weight * values, axis=0) / jnp.maximum(weight_sum, 1.0)
    spread = jnp.sum(weight * (values - average) ** 2, axis=0) / jnp.maximum(weight_sum - 1.0, 1.0)
    return (average, spread)


def apply_filter(averages, fringe_filter):
    result = jnp.dot(
        lax.all_gather(fringe_filter, "bl", axis=0, tiled=True),
        averages,
        preferred_element_type=jnp.float32,
    )
    return result.astype(jnp.bfloat16)


def shards(visibility, start_bin, coverage, clip_flags, fringe_filter):
    lst_count = lax.axis_size("lst")
    lst_index = lax.axis_index("lst")
    observed_night_count, binned_row_block, baseline_pairs, row_span_width = visibility.shape
    column_slots = baseline_pairs * row_span_width
    samples = visibility.reshape(observed_night_count, binned_row_block, column_slots)
    integration = lst_index * binned_row_block + jnp.arange(binned_row_block, dtype=jnp.int32)
    present_mask = integration[None, :] < coverage[:, None]
    usable = jnp.logical_and(present_mask[:, :, None], clip_flags == 0).astype(jnp.bfloat16)
    steps_over = start_bin // binned_row_block
    within = start_bin % binned_row_block
    current = (samples, usable)
    for bit_index in range((lst_count - 1).bit_length()):
        shifted = from_behind((current[0], current[1]), "lst", 1 << bit_index)
        chosen = steps_over >> bit_index & 1 == 1
        current = (
            jnp.where(chosen[:, None, None], shifted[0], current[0]),
            jnp.where(chosen[:, None, None], shifted[1], current[1]),
        )
    earlier = from_behind((current[0], current[1]), "lst", 1)
    offsets = binned_row_block - within
    slider = jax.vmap(partial(slide_rows, length=binned_row_block))
    aligned = slider(jnp.concatenate([earlier[0], current[0]], axis=1), offsets)
    weight = slider(jnp.concatenate([earlier[1], current[1]], axis=1), offsets)
    weight = jnp.broadcast_to(weight[:, :, :, None], weight.shape + (row_span_width,))
    weight = weight.reshape(observed_night_count, binned_row_block, column_slots).astype(
        jnp.float32
    )
    average, spread = statistic_moments(aligned, weight)
    by_column = lax.all_to_all(
        average.astype(jnp.bfloat16), "lst", split_axis=1, concat_axis=0, tiled=True
    )
    filtered = lax.all_to_all(
        apply_filter(by_column, fringe_filter), "lst", split_axis=0, concat_axis=1, tiled=True
    )
    spread = spread.astype(jnp.bfloat16)
    return (
        filtered.reshape(binned_row_block, baseline_pairs, row_span_width),
        spread.reshape(binned_row_block, baseline_pairs, row_span_width),
    )


def solution(mesh):
    placed = (P(None, "lst", "bl", None), P(), P(), P(None, "lst", "bl"), P("bl", None))
    return jax.shard_map(
        shards,
        mesh=mesh,
        in_specs=placed,
        out_specs=(P("lst", "bl", None), P("lst", "bl", None)),
        check_vma=False,
    )
```

profile of v0, /device:TPU:1, one launch (start us, length us, event | category | flops | bytes accessed | tf_op | source)
XLA Modules:
  0.0 495.1 jit_solution(15249125565116894148)
XLA Ops:
  7.2 5.8 %reshape.105 = bf16[4,32,12288]{2,1,0:T(8,128)(2,1)S(1)} reshape(bf16[4,32,4,3072]{3,2,1,0:T(4,128)(2,1)} %param.5) | data formatting | bytes 6291456 | tf_op jit(solution)/shard_map/reshape | solution.py:40
  13.0 2.7 collective-permute-start.6
  15.8 34.2 %collective-permute-done.6 = bf16[4,32,12288]{2,1,0:T(8,128)(2,1)S(1)} collective-permute-done((bf16[4,32,12288]{2,1,0:T(8,128)(2,1)S(1)}, bf16[4,32,12288]{2,1,0:T(8,128)(2,1)S(1)}, u32[]{:S(2)}, u32[]{:S(2)}) %collective-permute-start.6) | collective-permute-done | bytes 3145760 | tf_op jit(solution)/shard_map/ppermute | solution.py:11
  49.9 0.5 broadcast_select_fusion
  50.4 1.3 collective-permute-start.7
  51.7 66.3 %collective-permute-done.7 = bf16[4,32,12288]{2,1,0:T(8,128)(2,1)S(1)} collective-permute-done((bf16[4,32,12288]{2,1,0:T(8,128)(2,1)S(1)}, bf16[4,32,12288]{2,1,0:T(8,128)(2,1)S(1)}, u32[]{:S(2)}, u32[]{:S(2)}) %collective-permute-start.7) | collective-permute-done | bytes 3145760 | tf_op jit(solution)/shard_map/ppermute | solution.py:11
  118.4 2.9 collective-permute-start.8
  121.3 65.2 %collective-permute-done.8 = bf16[4,32,12288]{2,1,0:T(8,128)(2,1)S(1)} collective-permute-done((bf16[4,32,12288]{2,1,0:T(8,128)(2,1)S(1)}, bf16[4,32,12288]{2,1,0:T(8,128)(2,1)S(1)}, u32[]{:S(2)}, u32[]{:S(2)}) %collective-permute-start.8) | collective-permute-done | bytes 3145760 | tf_op jit(solution)/shard_map/ppermute | solution.py:11
  186.9 1.6 collective-permute-start.9
  188.5 66.5 %collective-permute-done.9 = bf16[4,32,12288]{2,1,0:T(8,128)(2,1)S(1)} collective-permute-done((bf16[4,32,12288]{2,1,0:T(8,128)(2,1)S(1)}, bf16[4,32,12288]{2,1,0:T(8,128)(2,1)S(1)}, u32[]{:S(2)}, u32[]{:S(2)}) %collective-permute-start.9) | collective-permute-done | bytes 3145760 | tf_op jit(solution)/shard_map/ppermute | solution.py:11
  255.4 2.9 collective-permute-start.10
  258.3 65.5 %collective-permute-done.10 = bf16[4,32,12288]{2,1,0:T(8,128)(2,1)S(1)} collective-permute-done((bf16[4,32,12288]{2,1,0:T(8,128)(2,1)S(1)}, bf16[4,32,12288]{2,1,0:T(8,128)(2,1)S(1)}, u32[]{:S(2)}, u32[]{:S(2)}) %collective-permute-start.10) | collective-permute-done | bytes 3145760 | tf_op jit(solution)/shard_map/ppermute | solution.py:11
  324.2 8.0 %collective-permute-start.11 = (bf16[4,32,12288]{2,1,0:T(8,128)(2,1)S(1)}, bf16[4,32,12288]{2,1,0:T(8,128)(2,1)}, u32[]{:S(2)}, u32[]{:S(2)}) collective-permute-start(bf16[4,32,12288]{2,1,0:T(8,128)(2,1)S(1)} %broadcast_select_fusion.4), channel_id=1, source_target_pairs={{0,1},{1,2},{2,3},{3,4},{4,5},{5,6},{6,7},{7,8},{8,9},{9,10},{10,1... | collective-permute-start | bytes 9437192 | tf_op jit(solution)/shard_map/ppermute | solution.py:11
  332.5 33.9 %collective-permute-done = bf16[4,32,4]{1,2,0:T(4,128)(2,1)S(1)} collective-permute-done((bf16[4,32,4]{1,2,0:T(4,128)(2,1)S(1)}, bf16[4,32,4]{1,2,0:T(4,128)(2,1)S(1)}, u32[]{:S(2)}, u32[]{:S(2)}) %collective-permute-start) | collective-permute-done | bytes 1056 | tf_op jit(solution)/shard_map/ppermute | solution.py:11
  366.5 5.8 %collective-permute-done.1 = bf16[4,32,4]{1,2,0:T(4,128)(2,1)S(1)} collective-permute-done((bf16[4,32,4]{1,2,0:T(4,128)(2,1)S(1)}, bf16[4,32,4]{1,2,0:T(4,128)(2,1)S(1)}, u32[]{:S(2)}, u32[]{:S(2)}) %collective-permute-start.1) | collective-permute-done | bytes 1056 | tf_op jit(solution)/shard_map/ppermute | solution.py:11
  372.4 6.1 %collective-permute-done.2 = bf16[4,32,4]{1,2,0:T(4,128)(2,1)S(1)} collective-permute-done((bf16[4,32,4]{1,2,0:T(4,128)(2,1)S(1)}, bf16[4,32,4]{1,2,0:T(4,128)(2,1)S(1)}, u32[]{:S(2)}, u32[]{:S(2)}) %collective-permute-start.2) | collective-permute-done | bytes 1056 | tf_op jit(solution)/shard_map/ppermute | solution.py:11
  378.6 3.9 collective-permute-done.3
  382.6 3.9 collective-permute-done.4
  386.6 4.3 collective-permute-start.5
  391.1 4.3 collective-permute-done.5
  395.6 0.7 gather_fusion
  396.3 3.5 broadcast_in_dim.88
  399.8 8.4 %broadcast_in_dim.89 = f32[4,32,12288]{2,1,0:T(8,128)} reshape(f32[4,32,4,3072]{3,2,1,0:T(4,128)} %broadcast_in_dim.88) | data formatting | bytes 12582912 | tf_op jit(solution)/shard_map/broadcast_in_dim | solution.py:59
  408.4 5.0 %pad_maximum_fusion = bf16[4,64,12288]{2,1,0:T(8,128)(2,1)} fusion(bf16[4,32,12288]{2,1,0:T(8,128)(2,1)S(1)} %broadcast_select_fusion.4, bf16[4,32,12288]{2,1,0:T(8,128)(2,1)} %collective-permute-done.11), kind=kLoop, calls=%fused_computation.9 | loop fusion | flops 12582912 | bytes 12582912 | tf_op jit(solution)/shard_map/concatenate | solution.py:57
  413.5 16.4 %while.1 = (s32[]{:T(128)}, bf16[4,64,12288]{2,1,0:T(8,128)(2,1)}, s32[4,3]{1,0:T(4,128)S(1)}, bf16[4,32,12288]{2,1,0:T(8,128)(2,1)}, s32[]{:T(128)}) while((s32[]{:T(128)}, bf16[4,64,12288]{2,1,0:T(8,128)(2,1)}, s32[4,3]{1,0:T(4,128)S(1)}, bf16[4,32,12288]{2,1,0:T(8,128)(2,1)}, s32[]{:T(128)}) %tuple.33), condition=%wide.while_cond, body=%wide.while_body.sunk | while | flops 2 | bytes 1574505 | solution.py:15
  413.5 0.6 fusion.11
  414.1 3.5 dynamic-slice_dynamic-update-slice_fusion.2
  417.6 0.6 fusion.11
  418.2 3.5 dynamic-slice_dynamic-update-slice_fusion.2
  421.7 0.6 fusion.11
  422.3 3.5 dynamic-slice_dynamic-update-slice_fusion.2
  425.7 0.6 fusion.11
  426.3 3.5 dynamic-slice_dynamic-update-slice_fusion.2
  429.8 4.7 fusion
  435.0 1.1 copy.34
  436.2 9.9 %all-to-all-start = ((bf16[32,32,384]{2,0,1:T(8,128)(2,1)}), bf16[32,32,384]{2,0,1:T(8,128)(2,1)}, u32[]{:S(2)}, u32[]{:S(2)}) async-start(bf16[32,32,384]{2,0,1:T(8,128)(2,1)} %copy.34), calls=%async_computation | async-start | bytes 1572864 | tf_op jit(solution)/shard_map/all_to_all | solution.py:64
  446.1 1.1 reduce_sum.46
  447.6 2.1 copy.38
  449.6 10.8 %all-to-all-done = bf16[32,32,384]{2,0,1:T(8,128)(2,1)} async-done(((bf16[32,32,384]{2,0,1:T(8,128)(2,1)}), bf16[32,32,384]{2,0,1:T(8,128)(2,1)}, u32[]{:S(2)}, u32[]{:S(2)}) %all-to-all-start) | async-done | bytes 786464 | tf_op jit(solution)/shard_map/all_to_all | solution.py:64
  460.5 3.9 fusion.5
  464.4 2.3 copy.35
  466.6 4.8 all-to-all-start.1
  471.5 5.8 %fusion.3 = f32[32,12288]{1,0:T(8,128)} fusion(f32[4,32,12288]{2,1,0:T(8,128)} %broadcast_in_dim.89, bf16[4,32,12288]{2,1,0:T(8,128)(2,1)S(1)} %copy-done, f32[32,12288]{1,0:T(8,128)} %bitcast.31), kind=kLoop, calls=%fused_computation.8 | loop fusion | flops 7471104 | bytes 12582912 | tf_op jit(solution)/shard_map/reduce_sum | solution.py:22
  477.2 2.4 reduce_sum.49
  479.7 1.2 divide_convert_fusion
  480.9 4.9 all-to-all-done.1
  485.8 1.4 copy.36
  487.2 1.1 reshape.106
  (52 shorter events, 4.0 us)
Async XLA Ops:
  7.2 442.5 %all-gather.2.cloned.1.call-start = ((), (), s32[]{:S(2)}) async-start(), calls=%async_computation.2 | async-start | bytes 2359296 | tf_op jit(solution)/shard_map/all_gather | solution.py:28
  7.2 8.5 %copy-start.2 = (s32[4]{0:T(128)S(1)}, s32[4]{0:T(128)}, u32[]{:S(2)}) copy-start(s32[4]{0:T(128)} %param.6) | copy-start | bytes 52
  13.0 36.9 %collective-permute-start.6 = (bf16[4,32,12288]{2,1,0:T(8,128)(2,1)S(1)}, bf16[4,32,12288]{2,1,0:T(8,128)(2,1)S(1)}, u32[]{:S(2)}, u32[]{:S(2)}) collective-permute-start(bf16[4,32,12288]{2,1,0:T(8,128)(2,1)S(1)} %reshape.105), channel_id=1, source_target_pairs={{0,1},{1,2},{2,3},{3,4},{4,5},{5,6},{6,7},{7,8},{8,9},{9,10},{10,1... | collective-permute-start | bytes 9437192 | tf_op jit(solution)/shard_map/ppermute | solution.py:11
  50.4 67.6 %collective-permute-start.7 = (bf16[4,32,12288]{2,1,0:T(8,128)(2,1)S(1)}, bf16[4,32,12288]{2,1,0:T(8,128)(2,1)S(1)}, u32[]{:S(2)}, u32[]{:S(2)}) collective-permute-start(bf16[4,32,12288]{2,1,0:T(8,128)(2,1)S(1)} %broadcast_select_fusion), channel_id=1, source_target_pairs={{0,2},{1,3},{2,4},{3,5},{4,6},{5,7},{6,8},{7,9},{8,10},{9,11},{10,... | collective-permute-start | bytes 9437192 | tf_op jit(solution)/shard_map/ppermute | solution.py:11
  118.4 68.1 %collective-permute-start.8 = (bf16[4,32,12288]{2,1,0:T(8,128)(2,1)S(1)}, bf16[4,32,12288]{2,1,0:T(8,128)(2,1)S(1)}, u32[]{:S(2)}, u32[]{:S(2)}) collective-permute-start(bf16[4,32,12288]{2,1,0:T(8,128)(2,1)S(1)} %broadcast_select_fusion.1), channel_id=1, source_target_pairs={{0,4},{1,5},{2,6},{3,7},{4,8},{5,9},{6,10},{7,11},{8,12},{9,13},{1... | collective-permute-start | bytes 9437192 | tf_op jit(solution)/shard_map/ppermute | solution.py:11
  186.9 68.1 %collective-permute-start.9 = (bf16[4,32,12288]{2,1,0:T(8,128)(2,1)S(1)}, bf16[4,32,12288]{2,1,0:T(8,128)(2,1)S(1)}, u32[]{:S(2)}, u32[]{:S(2)}) collective-permute-start(bf16[4,32,12288]{2,1,0:T(8,128)(2,1)S(1)} %broadcast_select_fusion.2), channel_id=1, source_target_pairs={{0,8},{1,9},{2,10},{3,11},{4,12},{5,13},{6,14},{7,15},{8,16},{9,17... | collective-permute-start | bytes 9437192 | tf_op jit(solution)/shard_map/ppermute | solution.py:11
  255.4 68.4 %collective-permute-start.10 = (bf16[4,32,12288]{2,1,0:T(8,128)(2,1)S(1)}, bf16[4,32,12288]{2,1,0:T(8,128)(2,1)S(1)}, u32[]{:S(2)}, u32[]{:S(2)}) collective-permute-start(bf16[4,32,12288]{2,1,0:T(8,128)(2,1)S(1)} %broadcast_select_fusion.3), channel_id=1, source_target_pairs={{0,16},{1,17},{2,18},{3,19},{4,20},{5,21},{6,22},{7,23},{8,24},{9,... | collective-permute-start | bytes 9437192 | tf_op jit(solution)/shard_map/ppermute | solution.py:11
  323.8 8.4 %copy-start.3 = (s32[4]{0:T(128)S(1)}, s32[4]{0:T(128)}, u32[]{:S(2)}) copy-start(s32[4]{0:T(128)} %param.7) | copy-start | bytes 52
  323.8 8.4 %copy-start.1 = (s32[4,32,4]{1,2,0:T(4,128)S(1)}, s32[4,32,4]{1,2,0:T(4,128)}, u32[]{:S(2)}) copy-start(s32[4,32,4]{1,2,0:T(4,128)} %param.8) | copy-start | bytes 6148
  324.2 84.3 %collective-permute-start.11 = (bf16[4,32,12288]{2,1,0:T(8,128)(2,1)S(1)}, bf16[4,32,12288]{2,1,0:T(8,128)(2,1)}, u32[]{:S(2)}, u32[]{:S(2)}) collective-permute-start(bf16[4,32,12288]{2,1,0:T(8,128)(2,1)S(1)} %broadcast_select_fusion.4), channel_id=1, source_target_pairs={{0,1},{1,2},{2,3},{3,4},{4,5},{5,6},{6,7},{7,8},{8,9},{9,10},{10,1... | collective-permute-start | bytes 9437192 | tf_op jit(solution)/shard_map/ppermute | solution.py:11
  332.2 34.2 %collective-permute-start = (bf16[4,32,4]{1,2,0:T(4,128)(2,1)S(1)}, bf16[4,32,4]{1,2,0:T(4,128)(2,1)S(1)}, u32[]{:S(2)}, u32[]{:S(2)}) collective-permute-start(bf16[4,32,4]{1,2,0:T(4,128)(2,1)S(1)} %and_convert_fusion), channel_id=1, source_target_pairs={{0,1},{1,2},{2,3},{3,4},{4,5},{5,6},{6,7},{7,8},{8,9},{9,10},{10,1... | collective-permute-start | bytes 3080 | tf_op jit(solution)/shard_map/ppermute | solution.py:11
  366.5 5.8 %collective-permute-start.1 = (bf16[4,32,4]{1,2,0:T(4,128)(2,1)S(1)}, bf16[4,32,4]{1,2,0:T(4,128)(2,1)S(1)}, u32[]{:S(2)}, u32[]{:S(2)}) collective-permute-start(bf16[4,32,4]{1,2,0:T(4,128)(2,1)S(1)} %broadcast_select_fusion.5), channel_id=1, source_target_pairs={{0,2},{1,3},{2,4},{3,5},{4,6},{5,7},{6,8},{7,9},{8,10},{9,11},{10,... | collective-permute-start | bytes 3080 | tf_op jit(solution)/shard_map/ppermute | solution.py:11
  372.3 6.1 %collective-permute-start.2 = (bf16[4,32,4]{1,2,0:T(4,128)(2,1)S(1)}, bf16[4,32,4]{1,2,0:T(4,128)(2,1)S(1)}, u32[]{:S(2)}, u32[]{:S(2)}) collective-permute-start(bf16[4,32,4]{1,2,0:T(4,128)(2,1)S(1)} %broadcast_select_fusion.6), channel_id=1, source_target_pairs={{0,4},{1,5},{2,6},{3,7},{4,8},{5,9},{6,10},{7,11},{8,12},{9,13},{1... | collective-permute-start | bytes 3080 | tf_op jit(solution)/shard_map/ppermute | solution.py:11
  378.5 4.0 collective-permute-start.3
  382.6 4.0 collective-permute-start.4
  386.6 8.7 %collective-permute-start.5 = (bf16[4,32,4]{1,2,0:T(4,128)(2,1)S(1)}, bf16[4,32,4]{1,2,0:T(4,128)(2,1)S(1)}, u32[]{:S(2)}, u32[]{:S(2)}) collective-permute-start(bf16[4,32,4]{1,2,0:T(4,128)(2,1)S(1)} %broadcast_select_fusion.9), channel_id=1, source_target_pairs={{0,1},{1,2},{2,3},{3,4},{4,5},{5,6},{6,7},{7,8},{8,9},{9,10},{10,1... | collective-permute-start | bytes 3080 | tf_op jit(solution)/shard_map/ppermute | solution.py:11
  436.2 24.3 %all-to-all-start = ((bf16[32,32,384]{2,0,1:T(8,128)(2,1)}), bf16[32,32,384]{2,0,1:T(8,128)(2,1)}, u32[]{:S(2)}, u32[]{:S(2)}) async-start(bf16[32,32,384]{2,0,1:T(8,128)(2,1)} %copy.34), calls=%async_computation | async-start | bytes 1572864 | tf_op jit(solution)/shard_map/all_to_all | solution.py:64
  460.5 11.0 %copy-start = (bf16[4,32,12288]{2,1,0:T(8,128)(2,1)S(1)}, bf16[4,32,12288]{2,1,0:T(8,128)(2,1)}, u32[]{:S(2)}) copy-start(bf16[4,32,12288]{2,1,0:T(8,128)(2,1)} %get-tuple-element.9) | copy-start | bytes 9437188
  466.6 19.2 %all-to-all-start.1 = ((bf16[32,32,384]{2,1,0:T(8,128)(2,1)}), bf16[32,32,384]{2,1,0:T(8,128)(2,1)}, u32[]{:S(2)}, u32[]{:S(2)}) async-start(bf16[32,32,384]{2,1,0:T(8,128)(2,1)} %bitcast.33), calls=%async_computation.1 | async-start | bytes 1572864 | tf_op jit(solution)/shard_map/all_to_all | solution.py:67
Sparse Core Ops, SparseCore 0:
  378.7 43.1 all-gather.1
where the time goes:
time: 496 us; the launch traced here: 495 us
  waiting for transfers between devices  371 us (75%)
  local copies, waits for them, and re-layouts  46.9 us (9%)
  starting transfers between devices  38.7 us (8%)
  other arithmetic  20 us (4%)
  between operations  14.2 us (3%)
    ppermute x12, waiting for transfers between devices, from_behind(): lax.ppermute(shard, axis, [(i, (i + by) % devices) for i in range(devices)])  356 us
    ppermute x12, starting transfers between devices, from_behind(): lax.ppermute(shard, axis, [(i, (i + by) % devices) for i in range(devices)])  24 us
    gather x12, local copies, waits for them, and re-layouts  16.4 us
    broadcast_in_dim x2, local copies, waits for them, and re-layouts, shards(): jnp.broadcast_to(weight[:, :, :, None], weight.shape + (row_span_width,))  11.9 us
    all_to_all x1, waiting for transfers between devices, shards(): lax.all_to_all(average.astype(jnp.bfloat16), 'lst', split_axis=1, concat_...  10.8 us
  transfers between devices with their start and end apart: 15, of which 13 were waited for; matrix products, arithmetic and copies ran while one was open for 11% of the time, Pallas kernels for 0%

commit v1 on v0

v1 whole, which is shorter than its diff:
```python
import functools

import jax
import jax.numpy as jnp
from jax import lax
from jax.experimental import pallas as pl
from jax.experimental.pallas import tpu as pltpu
from jax.sharding import PartitionSpec as P

LANES = 128


def total_wait(ref, sem):
    pltpu.make_async_copy(ref, ref, sem).wait()


def kernel(
    sizes,
    start_ref,
    cover_ref,
    flags_ref,
    vis_hbm,
    filt_hbm,
    out_f,
    out_s,
    vis,
    stage,
    send_in,
    recv_in,
    w_send,
    w_recv,
    rows,
    w_rows,
    w_al,
    inv_mean,
    inv_var,
    filt,
    means,
    send_out,
    recv_out,
    vis_sem,
    in_send,
    in_recv,
    w_sems,
    f_send,
    f_recv,
    out_send,
    out_recv,
):
    nights, block, bls, lst_n, bl_n, tiles = sizes
    groups = lst_n // bls
    bins = block * lst_n
    me = lax.axis_index("lst")
    zed = lax.axis_index("bl")
    core = lax.rem(me, 2)
    partner = me + 1 - 2 * core
    my_b, my_g = me // groups, lax.rem(me, groups)
    half = filt.shape[2]

    barrier = pltpu.get_barrier_semaphore()

    def greet_lst(i, _):
        pl.semaphore_signal(barrier, 1, device_id={"lst": lax.rem(me + i, lst_n)})
        return 0

    def greet_bl(i, _):
        pl.semaphore_signal(barrier, 1, device_id={"bl": lax.rem(zed + i, bl_n)})
        return 0

    load = pltpu.make_async_copy(vis_hbm, vis, vis_sem)
    load.start()
    lax.fori_loop(1, lst_n, greet_lst, 0)
    lax.fori_loop(1, bl_n, greet_bl, 0)

    own_half = pltpu.make_async_copy(
        filt_hbm.at[pl.ds(pl.multiple_of(core * half, half), half)],
        filt.at[zed, core],
        f_recv.at[0],
    )
    own_half.start()

    lane = lax.broadcasted_iota(jnp.int32, (1, block), 1) + me * block
    w_send[...] = jnp.zeros_like(w_send)
    for n in range(nights):
        seen = lane < cover_ref[n]
        for b in range(bls):
            good = jnp.logical_and(seen, flags_ref[n, b : b + 1, :] == 0)
            w_send[b, n : n + 1, 0:block] = jnp.where(good, 1.0, 0.0).astype(jnp.float32)

    load.wait()

    def regroup(tile, group):
        lanes = pl.ds(pl.multiple_of((group * tiles + tile) * LANES, LANES), LANES)
        for n in range(nights):
            for t in range(block):
                stage[n, t * bls : (t + 1) * bls, :] = vis[n, t, :, lanes].astype(jnp.float32)
            for b in range(bls):
                piece = stage[n, pl.ds(b, block, stride=bls), :]
                send_in[tile, b * groups + group, n] = piece.astype(jnp.bfloat16)

    def order(step):
        far = (step + 1) // 2
        return lax.rem(my_g + jnp.where(lax.rem(step, 2) == 1, far, groups - far), groups)

    def send_group(tile, group):
        for i in (1, 3, 2, 0):
            b = lax.rem(my_b + i, bls)
            q = b * groups + group

            def remote():
                pltpu.make_async_remote_copy(
                    send_in.at[tile, q],
                    recv_in.at[tile, me],
                    in_send.at[tile],
                    in_recv.at[tile],
                    device_id={"lst": q},
                ).start()

            if i == 0:
                pl.when(group != my_g)(remote)

                @pl.when(group == my_g)
                def _():
                    pltpu.make_async_copy(
                        send_in.at[tile, q], recv_in.at[tile, me], in_recv.at[tile]
                    ).start()
            else:
                remote()

    regroup(0, order(0))
    pl.semaphore_wait(barrier, lst_n - 1 + bl_n - 1)
    send_group(0, order(0))

    def send_half(i, _):
        pltpu.make_async_remote_copy(
            filt_hbm.at[pl.ds(pl.multiple_of(core * half, half), half)],
            filt.at[zed, core],
            f_send.at[0],
            f_recv.at[0],
            device_id={"bl": lax.rem(zed + i, bl_n)},
        ).start()
        return 0

    lax.fori_loop(1, bl_n, send_half, 0)

    def send_weights(i, _):
        q = lax.rem(me + i, lst_n)
        pltpu.make_async_remote_copy(
            w_send.at[q // groups], w_recv.at[me], w_sems.at[0], w_sems.at[1], device_id={"lst": q}
        ).start()
        return 0

    lax.fori_loop(1, lst_n, send_weights, 0)
    pltpu.make_async_copy(w_send.at[my_b], w_recv.at[me], w_sems.at[1]).start()

    def send_step(step, _):
        tile = step // groups
        group = order(lax.rem(step, groups))
        regroup(tile, group)
        send_group(tile, group)
        return 0

    lax.fori_loop(1, tiles * groups, send_step, 0)

    total_wait(w_recv, w_sems.at[1])
    shape = (block, LANES)
    diagonal = lax.broadcasted_iota(jnp.int32, shape, 0) == lax.broadcasted_iota(
        jnp.int32, shape, 1
    )

    def spread_weights(src, _):
        for n in range(nights):
            row = jnp.broadcast_to(w_recv[src, n : n + 1, :], shape)
            column = jnp.sum(jnp.where(diagonal, row, 0.0), axis=1, keepdims=True)
            at = pl.ds(pl.multiple_of(src * block, block), block)
            w_rows[n, at, :] = jnp.broadcast_to(column, shape)
        return 0

    lax.fori_loop(0, lst_n, spread_weights, 0)
    for n in range(nights):
        w_rows[n, bins : bins + block, :] = w_rows[n, 0:block, :]

    def first_row(n, k):
        return lax.rem(k * block + bins - start_ref[n], bins)

    def align_weights(k, _):
        at = pl.ds(pl.multiple_of(k * block, block), block)
        count = jnp.zeros(shape, jnp.float32)
        for n in range(nights):
            w = w_rows[n, pl.ds(first_row(n, k), block), :]
            w_al[n, at, :] = w
            count = count + w
        inv_mean[at, :] = 1.0 / jnp.maximum(count, 1.0)
        inv_var[at, :] = 1.0 / jnp.maximum(count - 1.0, 1.0)
        return 0

    lax.fori_loop(0, lst_n, align_weights, 0)

    total_wait(filt.at[:, core], f_recv.at[0])
    swap = pltpu.make_async_remote_copy(
        filt.at[:, core],
        filt.at[:, core],
        f_send.at[1],
        f_recv.at[1],
        device_id={"lst": partner},
    )
    swap.start()

    def bin_tile(tile, _):
        total_wait(recv_in.at[tile], in_recv.at[tile])

        def widen(src, _):
            at = pl.ds(pl.multiple_of(src * block, block), block)
            for n in range(nights):
                rows[n, at, :] = recv_in[tile, src, n].astype(jnp.float32)
            return 0

        lax.fori_loop(0, lst_n, widen, 0)
        for n in range(nights):
            rows[n, bins : bins + block, :] = rows[n, 0:block, :]

        def moments(k, _):
            at = pl.ds(pl.multiple_of(k * block, block), block)
            x = [rows[n, pl.ds(first_row(n, k), block), :] for n in range(nights)]
            w = [w_al[n, at, :] for n in range(nights)]
            total = x[0] * w[0]
            for n in range(1, nights):
                total = total + x[n] * w[n]
            mean = total * inv_mean[at, :]
            square = jnp.zeros(shape, jnp.float32)
            for n in range(nights):
                off = x[n] - mean
                square = square + w[n] * (off * off)
            means[at, :] = mean.astype(jnp.bfloat16)
            send_out[tile, k, 1] = (square * inv_var[at, :]).astype(jnp.bfloat16)
            return 0

        lax.fori_loop(0, lst_n, moments, 0)

        @pl.when(tile == 0)
        def _():
            total_wait(filt.at[:, 1 - core], f_recv.at[1])

        def apply_filter(z, _):
            product = jnp.dot(
                filt[z].reshape(2 * half, bins), means[...], preferred_element_type=jnp.float32
            ).astype(jnp.bfloat16)
            per = 2 * half // block
            for r in range(per):
                send_out[tile, z * per + r, 0] = product[r * block : (r + 1) * block, :]
            return 0

        lax.fori_loop(0, bl_n, apply_filter, 0)

        def send_back(i, _):
            q = lax.rem(me + i, lst_n)
            pltpu.make_async_remote_copy(
                send_out.at[tile, q],
                recv_out.at[tile, me],
                out_send.at[tile],
                out_recv.at[tile],
                device_id={"lst": q},
            ).start()
            return 0

        lax.fori_loop(1, lst_n, send_back, 0)
        pltpu.make_async_copy(
            send_out.at[tile, me], recv_out.at[tile, me], out_recv.at[tile]
        ).start()
        return 0

    lax.fori_loop(0, tiles, bin_tile, 0)

    def place_tile(tile, _):
        total_wait(recv_out.at[tile], out_recv.at[tile])

        def place(group, _):
            lanes = pl.ds(pl.multiple_of((group * tiles + tile) * LANES, LANES), LANES)
            for which, out in ((0, out_f), (1, out_s)):
                for b in range(bls):
                    stage[which, pl.ds(b, block, stride=bls), :] = recv_out[
                        tile, b * groups + group, which
                    ].astype(jnp.float32)
                for t in range(block):
                    out[t, :, lanes] = stage[which, t * bls : (t + 1) * bls, :].astype(
                        jnp.bfloat16
                    )
            return 0

        lax.fori_loop(0, groups, place, 0)
        return 0

    lax.fori_loop(0, tiles, place_tile, 0)

    for tile in range(tiles):
        total_wait(send_in.at[tile, pl.ds(0, lst_n - 1)], in_send.at[tile])
        total_wait(send_out.at[tile, pl.ds(0, lst_n - 1)], out_send.at[tile])
    total_wait(w_recv.at[pl.ds(0, lst_n - 1)], w_sems.at[0])
    total_wait(filt.at[pl.ds(0, bl_n - 1), 0], f_send.at[0])
    total_wait(filt.at[:, 0], f_send.at[1])


def shards(visibility, start_bin, coverage, clip_flags, fringe_filter):
    lst_n, bl_n = lax.axis_size("lst"), lax.axis_size("bl")
    nights, block, bls, width = visibility.shape
    rows, bins = fringe_filter.shape
    groups = lst_n // bls
    tiles = width // (groups * LANES)
    sizes = (nights, block, bls, lst_n, bl_n, tiles)
    bf16, f32 = jnp.bfloat16, jnp.float32
    out = jax.ShapeDtypeStruct((block, bls, width), bf16)
    smem = pl.BlockSpec(memory_space=pltpu.SMEM)
    vmem = pl.BlockSpec(memory_space=pltpu.VMEM)
    hbm = pl.BlockSpec(memory_space=pl.ANY)
    dma = pltpu.SemaphoreType.DMA
    return pl.pallas_call(
        functools.partial(kernel, sizes),
        out_shape=(out, out),
        in_specs=[smem, smem, vmem, hbm, hbm],
        out_specs=(vmem, vmem),
        scratch_shapes=[
            pltpu.VMEM(visibility.shape, bf16),
            pltpu.VMEM((nights, block * bls, LANES), f32),
            pltpu.VMEM((tiles, lst_n, nights, block, LANES), bf16),
            pltpu.VMEM((tiles, lst_n, nights, block, LANES), bf16),
            pltpu.VMEM((bls, nights, LANES), f32),
            pltpu.VMEM((lst_n, nights, LANES), f32),
            pltpu.VMEM((nights, bins + block, LANES), f32),
            pltpu.VMEM((nights, bins + block, LANES), f32),
            pltpu.VMEM((nights, bins, LANES), f32),
            pltpu.VMEM((bins, LANES), f32),
            pltpu.VMEM((bins, LANES), f32),
            pltpu.VMEM((bl_n, 2, rows // 2, bins), bf16),
            pltpu.VMEM((bins, LANES), bf16),
            pltpu.VMEM((tiles, lst_n, 2, block, LANES), bf16),
            pltpu.VMEM((tiles, lst_n, 2, block, LANES), bf16),
            dma,
            dma((tiles,)),
            dma((tiles,)),
            dma((2,)),
            dma((2,)),
            dma((2,)),
            dma((tiles,)),
            dma((tiles,)),
        ],
        compiler_params=pltpu.CompilerParams(
            collective_id=0, has_side_effects=True, vmem_limit_bytes=48 * 2**20
        ),
        cost_estimate=pl.CostEstimate(
            flops=2 * bins * bins * tiles * LANES, bytes_accessed=8 * 2**20, transcendentals=0
        ),
    )(start_bin, coverage, jnp.swapaxes(clip_flags, 1, 2), visibility, fringe_filter)


def solution(mesh):
    placed = (P(None, "lst", "bl", None), P(), P(), P(None, "lst", "bl"), P("bl", None))
    return jax.shard_map(
        shards,
        mesh=mesh,
        in_specs=placed,
        out_specs=(P("lst", "bl", None), P("lst", "bl", None)),
        check_vma=False,
    )
```

time: 496 us -> 73.1 us (0.15)
  waiting for transfers between devices: 371 us -> 0 us
  Pallas kernels: 0 us -> 65.6 us
  local copies, waits for them, and re-layouts: 46.9 us -> 6.6 us
  starting transfers between devices: 38.7 us -> 0 us
  other arithmetic: 20 us -> 0 us
  between operations: 14.2 us -> 0.65 us
    ppermute x12 -> x0, waiting for transfers between devices: 356 us -> none  [from_behind(): lax.ppermute(shard, axis, [(i, (i + by) % devices) for i in range(devices)])]
    pallas_call x0 -> x1, Pallas kernels: none -> 65.6 us  [shards(): pl.pallas_call(functools.partial(kernel, sizes), out_shape=(out, out), in...]
    ppermute x12 -> x0, starting transfers between devices: 24 us -> none  [from_behind(): lax.ppermute(shard, axis, [(i, (i + by) % devices) for i in range(devices)])]
    gather x14 -> x0, local copies, waits for them, and re-layouts: 17.1 us -> none
    all_to_all x2 -> x0, waiting for transfers between devices: 15.8 us -> none  [the longest x1 10.8 us: shards(): lax.all_to_all(average.astype(jnp.bfloat16), 'lst', split_axis=1, concat_...]
    all_to_all x2 -> x0, starting transfers between devices: 14.7 us -> none  [the longest x1 9.89 us: shards(): lax.all_to_all(average.astype(jnp.bfloat16), 'lst', split_axis=1, concat_...]
    broadcast_in_dim x2 -> x0, local copies, waits for them, and re-layouts: 11.9 us -> none  [shards(): jnp.broadcast_to(weight[:, :, :, None], weight.shape + (row_span_width,))]
    reduce_sum x3 -> x0, other arithmetic: 10.5 us -> none  [the longest x1 5.79 us: statistic_moments(): jnp.sum(weight * (values - average) ** 2, axis=0)]
  transfers between devices with their start and end apart: 15 -> 0, of which waited for: 13 -> 0; matrix products, arithmetic and copies ran while one was open for 11% -> 0% of each run, Pallas kernels for 0% -> 0%
where the time goes in v1:
time: 73.1 us; the launch traced here: 72.9 us
  Pallas kernels  65.6 us (90%)
  local copies, waits for them, and re-layouts  6.6 us (9%)
    pallas_call x1, Pallas kernels, shards(): pl.pallas_call(functools.partial(kernel, sizes), out_shape=(out, out), in...  65.6 us
    unnamed x12, local copies, waits for them, and re-layouts  6.6 us

profile of v1, /device:TPU:1, one launch (start us, length us, event | category | flops | bytes accessed | tf_op | source)
XLA Modules:
  0.0 72.9 jit_solution(12366207044019097919)
XLA Ops:
  0.6 0.0 copy-start
  0.6 1.9 %copy-done = bf16[4,32,4,3072]{3,2,1,0:T(4,128)(2,1)S(1)} copy-done((bf16[4,32,4,3072]{3,2,1,0:T(4,128)(2,1)S(1)}, bf16[4,32,4,3072]{3,2,1,0:T(4,128)(2,1)}, u32[]{:S(2)}) %copy-start) | copy-done | bytes 3145752
  2.5 0.0 copy-start.1
  2.5 0.9 %copy-done.1 = bf16[128,1024]{1,0:T(8,128)(2,1)S(1)} copy-done((bf16[128,1024]{1,0:T(8,128)(2,1)S(1)}, bf16[128,1024]{1,0:T(8,128)(2,1)}, u32[]{:S(2)}) %copy-start.1) | copy-done | bytes 262168
  3.5 0.0 copy-start.2
  3.5 0.7 copy-done.2
  4.2 0.0 copy-start.3
  4.2 0.7 copy-done.3
  4.8 0.0 copy-start.4
  4.8 0.7 copy-done.4
  5.5 65.6 %shard_map.68 = (bf16[32,4,3072]{2,1,0:T(4,128)(2,1)S(1)}, bf16[32,4,3072]{2,1,0:T(4,128)(2,1)S(1)}) custom-call(s32[4]{0:T(128)S(1)} %copy-done.3, s32[4]{0:T(128)S(1)} %copy-done.4, s32[4,4,32]{2,1,0:T(4,128)S(1)} %bitcast.1, bf16[4,32,4,3072]{3,2,1,0:T(4,128)(2,1)S(1)} %copy-done, bf16[128,1024]{1,0:T(8,128)(2,1)S(1)} %copy-done.1), custom_call_target="tpu_custom_call" | custom-call | flops 805306368 | bytes 8388608 | tf_op jit(solution)/shard_map/pallas_call | solution.py:316
  71.1 0.9 %copy.9 = bf16[32,4,3072]{2,1,0:T(4,128)(2,1)} copy(bf16[32,4,3072]{2,1,0:T(4,128)(2,1)S(1)} %get-tuple-element.4) | data formatting | bytes 1572864
  72.0 0.9 %copy.10 = bf16[32,4,3072]{2,1,0:T(4,128)(2,1)} copy(bf16[32,4,3072]{2,1,0:T(4,128)(2,1)S(1)} %get-tuple-element.5) | data formatting | bytes 1572864
Async XLA Ops:
  0.6 1.9 %copy-start = (bf16[4,32,4,3072]{3,2,1,0:T(4,128)(2,1)S(1)}, bf16[4,32,4,3072]{3,2,1,0:T(4,128)(2,1)}, u32[]{:S(2)}) copy-start(bf16[4,32,4,3072]{3,2,1,0:T(4,128)(2,1)} %vis_hbm.1) | copy-start | bytes 9437188
  2.5 0.9 %copy-start.1 = (bf16[128,1024]{1,0:T(8,128)(2,1)S(1)}, bf16[128,1024]{1,0:T(8,128)(2,1)}, u32[]{:S(2)}) copy-start(bf16[128,1024]{1,0:T(8,128)(2,1)} %filt_hbm.1) | copy-start | bytes 786436
  3.5 0.7 copy-start.2
  4.2 0.7 copy-start.3
  4.8 0.7 copy-start.4

commit v2 on v1

--- a/solution.py
+++ b/solution.py
@@ -16,13 +16,16 @@
 
 def kernel(
     sizes,
-    start_ref,
-    cover_ref,
-    flags_ref,
+    start_hbm,
+    cover_hbm,
+    flags_hbm,
     vis_hbm,
     filt_hbm,
     out_f,
     out_s,
+    start_ref,
+    cover_ref,
+    flags_ref,
     vis,
     stage,
     send_in,
@@ -39,6 +42,7 @@
     send_out,
     recv_out,
     vis_sem,
+    small_sems,
     in_send,
     in_recv,
     w_sems,
@@ -68,6 +72,14 @@
         return 0
 
     load = pltpu.make_async_copy(vis_hbm, vis, vis_sem)
+    small = [
+        pltpu.make_async_copy(src, dst, small_sems.at[i])
+        for i, (src, dst) in enumerate(
+            ((start_hbm, start_ref), (cover_hbm, cover_ref), (flags_hbm, flags_ref))
+        )
+    ]
+    for copy in small:
+        copy.start()
     load.start()
     lax.fori_loop(1, lst_n, greet_lst, 0)
     lax.fori_loop(1, bl_n, greet_bl, 0)
@@ -78,6 +90,9 @@
         f_recv.at[0],
     )
     own_half.start()
+
+    for copy in small:
+        copy.wait()
 
     lane = lax.broadcasted_iota(jnp.int32, (1, block), 1) + me * block
     w_send[...] = jnp.zeros_like(w_send)
@@ -309,16 +324,18 @@
     sizes = (nights, block, bls, lst_n, bl_n, tiles)
     bf16, f32 = jnp.bfloat16, jnp.float32
     out = jax.ShapeDtypeStruct((block, bls, width), bf16)
-    smem = pl.BlockSpec(memory_space=pltpu.SMEM)
     vmem = pl.BlockSpec(memory_space=pltpu.VMEM)
-    hbm = pl.BlockSpec(memory_space=pl.ANY)
+    hbm = pl.BlockSpec(memory_space=pltpu.HBM)
     dma = pltpu.SemaphoreType.DMA
     return pl.pallas_call(
         functools.partial(kernel, sizes),
         out_shape=(out, out),
-        in_specs=[smem, smem, vmem, hbm, hbm],
+        in_specs=[hbm] * 5,
         out_specs=(vmem, vmem),
         scratch_shapes=[
+            pltpu.SMEM((nights,), jnp.int32),
+            pltpu.SMEM((nights,), jnp.int32),
+            pltpu.VMEM((nights, bls, block), jnp.int32),
             pltpu.VMEM(visibility.shape, bf16),
             pltpu.VMEM((nights, block * bls, LANES), f32),
             pltpu.VMEM((tiles, lst_n, nights, block, LANES), bf16),
@@ -335,6 +352,7 @@
             pltpu.VMEM((tiles, lst_n, 2, block, LANES), bf16),
             pltpu.VMEM((tiles, lst_n, 2, block, LANES), bf16),
             dma,
+            dma((3,)),
             dma((tiles,)),
             dma((tiles,)),
             dma((2,)),
@@ -349,7 +367,18 @@
         cost_estimate=pl.CostEstimate(
             flops=2 * bins * bins * tiles * LANES, bytes_accessed=8 * 2**20, transcendentals=0
         ),
-    )(start_bin, coverage, jnp.swapaxes(clip_flags, 1, 2), visibility, fringe_filter)
+    )(
+        *[
+            pltpu.with_memory_space_constraint(x, pltpu.HBM)
+            for x in (
+                start_bin,
+                coverage,
+                jnp.swapaxes(clip_flags, 1, 2),
+                visibility,
+                fringe_filter,
+            )
+        ]
+    )
 
 
 def solution(mesh):

time: 73.1 us -> 67.4 us (0.922)
  local copies, waits for them, and re-layouts: 6.6 us -> 1.76 us
    unnamed x12 -> x2, local copies, waits for them, and re-layouts: 6.6 us -> 1.76 us
where the time goes in v2:
time: 67.4 us; the launch traced here: 67.3 us
  Pallas kernels  64.9 us (96%)
  local copies, waits for them, and re-layouts  1.76 us (3%)
    pallas_call x1, Pallas kernels, shards(): pl.pallas_call(functools.partial(kernel, sizes), out_shape=(out, out), in...  64.9 us
    unnamed x2, local copies, waits for them, and re-layouts  1.76 us

profile of v2, /device:TPU:1, one launch (start us, length us, event | category | flops | bytes accessed | tf_op | source)
XLA Modules:
  0.0 67.3 jit_solution(445026736966264827)
XLA Ops:
  0.6 64.9 %shard_map.68 = (bf16[32,4,3072]{2,1,0:T(4,128)(2,1)S(1)}, bf16[32,4,3072]{2,1,0:T(4,128)(2,1)S(1)}) custom-call(s32[4]{0:T(128)} %start_hbm.1, s32[4]{0:T(128)} %cover_hbm.1, s32[4,4,32]{2,1,0:T(4,128)} %bitcast.1, bf16[4,32,4,3072]{3,2,1,0:T(4,128)(2,1)} %vis_hbm.1, bf16[128,1024]{1,0:T(8,128)(2,1)} %filt_hbm.1), custom_call_target="tpu_custom_call" | custom-call | flops 805306368 | bytes 8388608 | tf_op jit(solution)/shard_map/pallas_call | solution.py:330
  65.5 0.9 %copy.9 = bf16[32,4,3072]{2,1,0:T(4,128)(2,1)} copy(bf16[32,4,3072]{2,1,0:T(4,128)(2,1)S(1)} %get-tuple-element.4) | data formatting | bytes 1572864
  66.4 0.9 %copy.10 = bf16[32,4,3072]{2,1,0:T(4,128)(2,1)} copy(bf16[32,4,3072]{2,1,0:T(4,128)(2,1)S(1)} %get-tuple-element.5) | data formatting | bytes 1572864

commit v3 on v2

v3 whole, which is shorter than its diff:
```python
import functools

import jax
import jax.numpy as jnp
from jax import lax
from jax.experimental import pallas as pl
from jax.experimental.pallas import tpu as pltpu
from jax.sharding import PartitionSpec as P

LANES = 128


def total_wait(ref, sem):
    pltpu.make_async_copy(ref, ref, sem).wait()


def kernel(
    sizes,
    start_hbm,
    cover_hbm,
    flags_hbm,
    vis_hbm,
    filt_hbm,
    out_f,
    out_s,
    start_ref,
    cover_ref,
    flags_ref,
    vis,
    stage,
    send_in,
    recv_in,
    w_send,
    w_recv,
    rows,
    w_rows,
    w_al,
    inv_mean,
    inv_var,
    filt,
    means,
    send_out,
    recv_out,
    plane_sem,
    vis_sems,
    small_sems,
    in_send,
    in_recv,
    w_sems,
    f_own,
    f_up_send,
    f_up,
    f_down_send,
    f_down,
    f_swap,
    out_send,
    out_recv,
):
    nights, block, bls, lst_n, bl_n, tiles = sizes
    groups = lst_n // bls
    bins = block * lst_n
    wide = groups * LANES
    me = lax.axis_index("lst")
    zed = lax.axis_index("bl")
    my_b, my_g = me // groups, lax.rem(me, groups)
    core = lax.rem(me, 2)
    partner = me + 1 - 2 * core
    partner_g = my_g + 1 - 2 * core
    half = filt.shape[2]
    up, down = lax.rem(zed + 1, bl_n), lax.rem(zed + bl_n - 1, bl_n)
    up_hops, down_hops = bl_n // 2, (bl_n - 1) // 2

    small = [
        pltpu.make_async_copy(src, dst, small_sems.at[i])
        for i, (src, dst) in enumerate(
            ((start_hbm, start_ref), (cover_hbm, cover_ref), (flags_hbm, flags_ref))
        )
    ]
    loads = [
        pltpu.make_async_copy(
            vis_hbm.at[:, :, :, pl.ds(tile * wide, wide)], vis.at[tile], vis_sems.at[tile]
        )
        for tile in range(tiles)
    ]
    loads[0].start()

    barrier = pltpu.get_barrier_semaphore()
    greeted = 0
    for i in (2, 1, 3):
        for g in (my_g, partner_g):
            q = lax.rem(my_b + i, bls) * groups + g
            pl.semaphore_signal(barrier, 1, device_id={"lst": q})
            greeted += 1
    for i in (4, 5, 3, 2, 6, 1, 7):
        q = my_b * groups + lax.rem(my_g + i, groups)
        pl.semaphore_signal(barrier, 1, device_id={"lst": q})
        greeted += 1

    if bl_n > 1:
        pl.semaphore_signal(barrier, 1, device_id={"bl": down})
        greeted += 1

        @pl.when(up > 0)
        def _():
            pl.semaphore_signal(barrier, 1, device_id={"bl": up})

    for copy in small:
        copy.start()
    own_half = pltpu.make_async_copy(
        filt_hbm.at[pl.ds(pl.multiple_of(core * half, half), half)], filt.at[zed, core], f_own
    )
    own_half.start()
    for load in loads[1:]:
        load.start()

    def regroup(tile, group):
        lanes = pl.ds(pl.multiple_of(group * LANES, LANES), LANES)
        for n in range(nights):
            for t in range(block):
                stage[n, t * bls : (t + 1) * bls, :] = vis[tile, n, t, :, lanes].astype(
                    jnp.float32
                )
            for b in range(bls):
                piece = stage[n, pl.ds(b, block, stride=bls), :]
                send_in[tile, b * groups + group, n] = piece.astype(jnp.bfloat16)

    def order(step):
        far = (step + 1) // 2
        return lax.rem(my_g + jnp.where(lax.rem(step, 2) == 1, far, groups - far), groups)

    def send_one(tile, b, group):
        q = b * groups + group
        pltpu.make_async_remote_copy(
            send_in.at[tile, q],
            recv_in.at[tile, me],
            in_send.at[tile],
            in_recv.at[tile],
            device_id={"lst": q},
        ).start()

    def send_row(tile, group):
        @pl.when(group != my_g)
        def _():
            send_one(tile, my_b, group)

        @pl.when(group == my_g)
        def _():
            pltpu.make_async_copy(
                send_in.at[tile, me], recv_in.at[tile, me], in_recv.at[tile]
            ).start()

    def send_rest(tile, group):
        for i in (1, 3, 2):
            send_one(tile, lax.rem(my_b + i, bls), group)

    def send_half(source, to, send_sem, recv_sem):
        return pltpu.make_async_remote_copy(
            filt.at[source, core],
            filt.at[source, core],
            send_sem,
            recv_sem,
            device_id={"bl": to},
        )

    def give_half(source):
        pltpu.make_async_remote_copy(
            filt.at[source, core],
            filt.at[source, core],
            f_swap.at[0],
            f_swap.at[1],
            device_id={"lst": partner},
        ).start()

    def pass_half(hops):
        if hops > up_hops:
            return
        source = lax.rem(zed + bl_n - hops, bl_n)
        total_wait(filt.at[0, core], f_up.at[hops - 1])
        if hops < up_hops:
            send_half(source, up, f_up_send.at[hops], f_up.at[hops]).start()
        give_half(source)
        if hops == 1 and down_hops:

            @pl.when(zed == 0)
            def _():
                send_half(zed, down, f_down_send.at[0], f_down.at[0]).start()

        if hops <= down_hops:
            source = lax.rem(zed + hops, bl_n)
            total_wait(filt.at[0, core], f_down.at[hops - 1])
            if hops < down_hops:
                send_half(source, down, f_down_send.at[hops], f_down.at[hops]).start()
            give_half(source)

    loads[0].wait()
    regroup(0, order(0))
    own_half.wait()
    pl.semaphore_wait(barrier, greeted + (jnp.where(zed > 0, 1, 0) if bl_n > 1 else 0))

    for i in (4, 2, 6):
        q = my_b * groups + lax.rem(my_g + i, groups)
        pl.semaphore_signal(plane_sem, 1, device_id={"lst": q})

    if up_hops:
        send_half(zed, up, f_up_send.at[0], f_up.at[0]).start()
    if down_hops:

        @pl.when(zed > 0)
        def _():
            send_half(zed, down, f_down_send.at[0], f_down.at[0]).start()

    give_half(zed)

    def send_near(step, _):
        group = order(step)

        @pl.when(step > 0)
        def _():
            regroup(0, group)

        send_row(0, group)

        @pl.when(jnp.logical_or(group == my_g, group == partner_g))
        def _():
            send_rest(0, group)

        return 0

    lax.fori_loop(0, groups, send_near, 0)

    pl.semaphore_wait(plane_sem, 3)

    def send_far(step, _):
        group = order(step)

        @pl.when(jnp.logical_and(group != my_g, group != partner_g))
        def _():
            send_rest(0, group)

        return 0

    lax.fori_loop(0, groups, send_far, 0)

    pass_half(1)

    for copy in small:
        copy.wait()
    lane = lax.broadcasted_iota(jnp.int32, (1, block), 1) + me * block
    for b in range(bls):
        parts = []
        for n in range(nights):
            good = jnp.logical_and(lane < cover_ref[n], flags_ref[n, b : b + 1, :] == 0)
            parts.append(jnp.where(good, 1.0, 0.0).astype(jnp.float32))
        w_send[b] = jnp.concatenate(parts, axis=1)

    def send_weights(i, _):
        q = lax.rem(me + i, lst_n)
        pltpu.make_async_remote_copy(
            w_send.at[q // groups], w_recv.at[me], w_sems.at[0], w_sems.at[1], device_id={"lst": q}
        ).start()
        return 0

    lax.fori_loop(1, lst_n, send_weights, 0)
    pltpu.make_async_copy(w_send.at[my_b], w_recv.at[me], w_sems.at[1]).start()

    for tile in range(1, tiles):
        loads[tile].wait()

        def send_step(step, _):
            group = order(step)
            regroup(tile, group)
            send_row(tile, group)
            send_rest(tile, group)
            return 0

        lax.fori_loop(0, groups, send_step, 0)
        pass_half(1 + tile)

    total_wait(w_recv, w_sems.at[1])
    shape = (block, LANES)
    below_diagonal = lax.broadcasted_iota(jnp.int32, shape, 1) - lax.broadcasted_iota(
        jnp.int32, shape, 0
    )

    def spread_weights(src, _):
        row = jnp.broadcast_to(w_recv[src], shape)
        at = pl.ds(pl.multiple_of(src * block, block), block)
        for n in range(nights):
            own = jnp.where(below_diagonal == n * block, row, 0.0)
            w_rows[n, at, :] = jnp.broadcast_to(jnp.sum(own, axis=1, keepdims=True), shape)
        return 0

    lax.fori_loop(0, lst_n, spread_weights, 0)
    for hops in range(1 + tiles, up_hops + 1):
        pass_half(hops)
    for n in range(nights):
        w_rows[n, bins : bins + block, :] = w_rows[n, 0:block, :]

    def first_row(n, k):
        return lax.rem(k * block + bins - start_ref[n], bins)

    def align_weights(k, _):
        at = pl.ds(pl.multiple_of(k * block, block), block)
        count = jnp.zeros(shape, jnp.float32)
        for n in range(nights):
            w = w_rows[n, pl.ds(first_row(n, k), block), :]
            w_al[n, at, :] = w
            count = count + w
        inv_mean[at, :] = 1.0 / jnp.maximum(count, 1.0)
        inv_var[at, :] = 1.0 / jnp.maximum(count - 1.0, 1.0)
        return 0

    lax.fori_loop(0, lst_n, align_weights, 0)

    def bin_tile(tile):
        total_wait(recv_in.at[tile], in_recv.at[tile])

        def widen(src, _):
            at = pl.ds(pl.multiple_of(src * block, block), block)
            for n in range(nights):
                rows[n, at, :] = recv_in[tile, src, n].astype(jnp.float32)
            return 0

        lax.fori_loop(0, lst_n, widen, 0)
        for n in range(nights):
            rows[n, bins : bins + block, :] = rows[n, 0:block, :]

        def moments(k, _):
            at = pl.ds(pl.multiple_of(k * block, block), block)
            x = [rows[n, pl.ds(first_row(n, k), block), :] for n in range(nights)]
            w = [w_al[n, at, :] for n in range(nights)]
            total = x[0] * w[0]
            for n in range(1, nights):
                total = total + x[n] * w[n]
            mean = total * inv_mean[at, :]
            square = jnp.zeros(shape, jnp.float32)
            for n in range(nights):
                off = x[n] - mean
                square = square + w[n] * (off * off)
            means[at, tile * LANES : (tile + 1) * LANES] = mean.astype(jnp.bfloat16)
            send_out[tile, k, 1] = (square * inv_var[at, :]).astype(jnp.bfloat16)
            return 0

        lax.fori_loop(0, lst_n, moments, 0)

    def filter_tiles(first, last):
        def apply_filter(z, _):
            product = jnp.dot(
                filt[z].reshape(2 * half, bins),
                means[:, first * LANES : last * LANES],
                preferred_element_type=jnp.float32,
            ).astype(jnp.bfloat16)
            per = 2 * half // block
            for tile in range(first, last):
                lanes = slice((tile - first) * LANES, (tile - first + 1) * LANES)
                for r in range(per):
                    send_out[tile, z * per + r, 0] = product[r * block : (r + 1) * block, lanes]
            return 0

        lax.fori_loop(0, bl_n, apply_filter, 0)
        for tile in range(first, last):

            def send_back(i, _):
                q = lax.rem(me + i, lst_n)
                pltpu.make_async_remote_copy(
                    send_out.at[tile, q],
                    recv_out.at[tile, me],
                    out_send.at[tile],
                    out_recv.at[tile],
                    device_id={"lst": q},
                ).start()
                return 0

            lax.fori_loop(1, lst_n, send_back, 0)
            pltpu.make_async_copy(
                send_out.at[tile, me], recv_out.at[tile, me], out_recv.at[tile]
            ).start()

    for tile in range(tiles - 1):
        bin_tile(tile)
    total_wait(filt.at[:, 1 - core], f_swap.at[1])
    filter_tiles(0, tiles - 1)
    bin_tile(tiles - 1)
    filter_tiles(tiles - 1, tiles)

    def place_tile(tile, _):
        total_wait(recv_out.at[tile], out_recv.at[tile])

        def place(group, _):
            lanes = pl.ds(pl.multiple_of((tile * groups + group) * LANES, LANES), LANES)
            for which, out in ((0, out_f), (1, out_s)):
                for b in range(bls):
                    stage[which, pl.ds(b, block, stride=bls), :] = recv_out[
                        tile, b * groups + group, which
                    ].astype(jnp.float32)
                for t in range(block):
                    out[t, :, lanes] = stage[which, t * bls : (t + 1) * bls, :].astype(
                        jnp.bfloat16
                    )
            return 0

        lax.fori_loop(0, groups, place, 0)
        return 0

    lax.fori_loop(0, tiles, place_tile, 0)

    for tile in range(tiles):
        total_wait(send_in.at[tile, pl.ds(0, lst_n - 1)], in_send.at[tile])
        total_wait(send_out.at[tile, pl.ds(0, lst_n - 1)], out_send.at[tile])
    total_wait(w_recv.at[pl.ds(0, lst_n - 1)], w_sems.at[0])
    total_wait(filt.at[:, 0], f_swap.at[0])

    for hops in range(up_hops):
        total_wait(filt.at[0, 0], f_up_send.at[hops])
    for hops in range(down_hops):
        total_wait(filt.at[0, 0], f_down_send.at[hops])


def shards(visibility, start_bin, coverage, clip_flags, fringe_filter):
    lst_n, bl_n = lax.axis_size("lst"), lax.axis_size("bl")
    nights, block, bls, width = visibility.shape
    rows, bins = fringe_filter.shape
    groups = lst_n // bls
    tiles = width // (groups * LANES)
    sizes = (nights, block, bls, lst_n, bl_n, tiles)
    bf16, f32 = jnp.bfloat16, jnp.float32
    out = jax.ShapeDtypeStruct((block, bls, width), bf16)
    vmem = pl.BlockSpec(memory_space=pltpu.VMEM)
    hbm = pl.BlockSpec(memory_space=pltpu.HBM)
    dma = pltpu.SemaphoreType.DMA
    return pl.pallas_call(
        functools.partial(kernel, sizes),
        out_shape=(out, out),
        in_specs=[hbm] * 5,
        out_specs=(vmem, vmem),
        scratch_shapes=[
            pltpu.SMEM((nights,), jnp.int32),
            pltpu.SMEM((nights,), jnp.int32),
            pltpu.VMEM((nights, bls, block), jnp.int32),
            pltpu.VMEM((tiles, nights, block, bls, groups * LANES), bf16),
            pltpu.VMEM((nights, block * bls, LANES), f32),
            pltpu.VMEM((tiles, lst_n, nights, block, LANES), bf16),
            pltpu.VMEM((tiles, lst_n, nights, block, LANES), bf16),
            pltpu.VMEM((bls, 1, nights * block), f32),
            pltpu.VMEM((lst_n, 1, nights * block), f32),
            pltpu.VMEM((nights, bins + block, LANES), f32),
            pltpu.VMEM((nights, bins + block, LANES), f32),
            pltpu.VMEM((nights, bins, LANES), f32),
            pltpu.VMEM((bins, LANES), f32),
            pltpu.VMEM((bins, LANES), f32),
            pltpu.VMEM((bl_n, 2, rows // 2, bins), bf16),
            pltpu.VMEM((bins, tiles * LANES), bf16),
            pltpu.VMEM((tiles, lst_n, 2, block, LANES), bf16),
            pltpu.VMEM((tiles, lst_n, 2, block, LANES), bf16),
            pltpu.SemaphoreType.REGULAR,
            dma((tiles,)),
            dma((3,)),
            dma((tiles,)),
            dma((tiles,)),
            dma((2,)),
            dma,
            dma((bl_n,)),
            dma((bl_n,)),
            dma((bl_n,)),
            dma((bl_n,)),
            dma((2,)),
            dma((tiles,)),
            dma((tiles,)),
        ],
        compiler_params=pltpu.CompilerParams(
            collective_id=0, has_side_effects=True, vmem_limit_bytes=48 * 2**20
        ),
        cost_estimate=pl.CostEstimate(
            flops=2 * bins * bins * tiles * LANES, bytes_accessed=8 * 2**20, transcendentals=0
        ),
    )(
        *[
            pltpu.with_memory_space_constraint(x, pltpu.HBM)
            for x in (
                start_bin,
                coverage,
                jnp.swapaxes(clip_flags, 1, 2),
                visibility,
                fringe_filter,
            )
        ]
    )


def solution(mesh):
    placed = (P(None, "lst", "bl", None), P(), P(), P(None, "lst", "bl"), P("bl", None))
    return jax.shard_map(
        shards,
        mesh=mesh,
        in_specs=placed,
        out_specs=(P("lst", "bl", None), P("lst", "bl", None)),
        check_vma=False,
    )
```

time: 67.4 us -> 62.7 us (0.930)
  Pallas kernels: 64.9 us -> 60.2 us
    pallas_call x1, Pallas kernels: 64.9 us -> 60.2 us  [shards(): pl.pallas_call(functools.partial(kernel, sizes), out_shape=(out, out), in...]
where the time goes in v3:
time: 62.7 us; the launch traced here: 62.6 us
  Pallas kernels  60.2 us (96%)
  local copies, waits for them, and re-layouts  1.76 us (3%)
  between operations  0.64 us (1%)
    pallas_call x1, Pallas kernels, shards(): pl.pallas_call(functools.partial(kernel, sizes), out_shape=(out, out), in...  60.2 us
    unnamed x2, local copies, waits for them, and re-layouts  1.76 us

profile of v3, /device:TPU:1, one launch (start us, length us, event | category | flops | bytes accessed | tf_op | source)
XLA Modules:
  0.0 62.6 jit_solution(2879381671876128710)
XLA Ops:
  0.6 60.2 %shard_map.68 = (bf16[32,4,3072]{2,1,0:T(4,128)(2,1)S(1)}, bf16[32,4,3072]{2,1,0:T(4,128)(2,1)S(1)}) custom-call(s32[4]{0:T(128)} %start_hbm.1, s32[4]{0:T(128)} %cover_hbm.1, s32[4,4,32]{2,1,0:T(4,128)} %bitcast.1, bf16[4,32,4,3072]{3,2,1,0:T(4,128)(2,1)} %vis_hbm.1, bf16[128,1024]{1,0:T(8,128)(2,1)} %filt_hbm.1), custom_call_target="tpu_custom_call" | custom-call | flops 805306368 | bytes 8388608 | tf_op jit(solution)/shard_map/pallas_call | solution.py:431
  60.8 0.9 %copy.9 = bf16[32,4,3072]{2,1,0:T(4,128)(2,1)} copy(bf16[32,4,3072]{2,1,0:T(4,128)(2,1)S(1)} %get-tuple-element.4) | data formatting | bytes 1572864
  61.7 0.9 %copy.10 = bf16[32,4,3072]{2,1,0:T(4,128)(2,1)} copy(bf16[32,4,3072]{2,1,0:T(4,128)(2,1)S(1)} %get-tuple-element.5) | data formatting | bytes 1572864

commit v4 on v3

--- a/solution.py
+++ b/solution.py
@@ -8,6 +8,10 @@
 from jax.sharding import PartitionSpec as P
 
 LANES = 128
+FAR_TO_NEAR = (
+    ((2, 2), (2, 1), (2, 3), (1, 2), (3, 2), (1, 1), (3, 3), (1, 3), (3, 1))
+    + ((2, 0), (0, 2), (1, 0), (3, 0), (0, 1), (0, 3))
+)
 
 
 def total_wait(ref, sem):
@@ -21,8 +25,7 @@
     flags_hbm,
     vis_hbm,
     filt_hbm,
-    out_f,
-    out_s,
+    out,
     start_ref,
     cover_ref,
     flags_ref,
@@ -41,6 +44,7 @@
     means,
     send_out,
     recv_out,
+    pair_sem,
     plane_sem,
     vis_sems,
     small_sems,
@@ -82,28 +86,25 @@
         )
         for tile in range(tiles)
     ]
-    loads[0].start()
 
     barrier = pltpu.get_barrier_semaphore()
-    greeted = 0
+    greeted = 7
     for i in (2, 1, 3):
-        for g in (my_g, partner_g):
-            q = lax.rem(my_b + i, bls) * groups + g
-            pl.semaphore_signal(barrier, 1, device_id={"lst": q})
-            greeted += 1
-    for i in (4, 5, 3, 2, 6, 1, 7):
+        q = lax.rem(my_b + i, bls) * groups + my_g
+        pl.semaphore_signal(barrier, 1, device_id={"lst": q})
+    for i in (4, 2, 6):
         q = my_b * groups + lax.rem(my_g + i, groups)
         pl.semaphore_signal(barrier, 1, device_id={"lst": q})
-        greeted += 1
-
+    pl.semaphore_signal(barrier, 1, device_id={"lst": partner})
     if bl_n > 1:
-        pl.semaphore_signal(barrier, 1, device_id={"bl": down})
-        greeted += 1
-
-        @pl.when(up > 0)
-        def _():
-            pl.semaphore_signal(barrier, 1, device_id={"bl": up})
-
+        pl.when(zed < bl_n - 1)(
+            lambda: pl.semaphore_signal(barrier, 1, device_id={"bl": zed + 1})
+        )
+        pl.when(zed == 0)(
+            lambda: pl.semaphore_signal(barrier, 1, device_id={"bl": bl_n - 1})
+        )
+
+    loads[0].start()
     for copy in small:
         copy.start()
     own_half = pltpu.make_async_copy(
@@ -172,62 +173,89 @@
         ).start()
 
     def pass_half(hops):
-        if hops > up_hops:
-            return
-        source = lax.rem(zed + bl_n - hops, bl_n)
-        total_wait(filt.at[0, core], f_up.at[hops - 1])
-        if hops < up_hops:
-            send_half(source, up, f_up_send.at[hops], f_up.at[hops]).start()
-        give_half(source)
-        if hops == 1 and down_hops:
-
-            @pl.when(zed == 0)
-            def _():
-                send_half(zed, down, f_down_send.at[0], f_down.at[0]).start()
-
         if hops <= down_hops:
-            source = lax.rem(zed + hops, bl_n)
+            above = lax.rem(zed + hops, bl_n)
             total_wait(filt.at[0, core], f_down.at[hops - 1])
-            if hops < down_hops:
-                send_half(source, down, f_down_send.at[hops], f_down.at[hops]).start()
-            give_half(source)
+            if hops == 1:
+                pl.when(zed < bl_n - 1)(own_up)
+
+            def on_down():
+                send_half(above, down, f_down_send.at[hops], f_down.at[hops]).start()
+
+            if 1 < hops < down_hops:
+                on_down()
+            elif hops < down_hops:
+                pl.when(zed > 0)(on_down)
+            give_half(above)
+        if hops <= up_hops:
+            below = lax.rem(zed + bl_n - hops, bl_n)
+            total_wait(filt.at[0, core], f_up.at[hops - 1])
+            if hops == 1:
+                pl.when(zed == 0)(own_down)
+                if hops < down_hops:
+                    pl.when(zed == 0)(on_down)
+            if hops < up_hops:
+                send_half(below, up, f_up_send.at[hops], f_up.at[hops]).start()
+            give_half(below)
 
     loads[0].wait()
     regroup(0, order(0))
     own_half.wait()
-    pl.semaphore_wait(barrier, greeted + (jnp.where(zed > 0, 1, 0) if bl_n > 1 else 0))
+    if bl_n > 1:
+        greeted += jnp.where(zed > 0, 1, 0) + jnp.where(zed == bl_n - 1, 1, 0)
+    pl.semaphore_wait(barrier, greeted)
+
+    pl.semaphore_signal(pair_sem, 1, device_id={"lst": partner})
+
+    def own_up():
+        send_half(zed, up, f_up_send.at[0], f_up.at[0]).start()
+
+    def own_down():
+        send_half(zed, down, f_down_send.at[0], f_down.at[0]).start()
+
+    if bl_n > 1:
+        pl.when(zed == bl_n - 1)(own_up)
+        pl.when(zed > 0)(own_down)
+    give_half(zed)
+
+    def send_near(step, _):
+        group = order(step)
+
+        @pl.when(step > 0)
+        def _():
+            regroup(0, group)
+
+        @pl.when(jnp.logical_or(lax.rem(group, 2) == core, group == partner_g))
+        def _():
+            send_row(0, group)
+
+        @pl.when(group == my_g)
+        def _():
+            send_rest(0, group)
+
+        return 0
+
+    lax.fori_loop(0, groups, send_near, 0)
+    pl.semaphore_wait(pair_sem, 1)
 
     for i in (4, 2, 6):
         q = my_b * groups + lax.rem(my_g + i, groups)
         pl.semaphore_signal(plane_sem, 1, device_id={"lst": q})
 
-    if up_hops:
-        send_half(zed, up, f_up_send.at[0], f_up.at[0]).start()
-    if down_hops:
-
-        @pl.when(zed > 0)
-        def _():
-            send_half(zed, down, f_down_send.at[0], f_down.at[0]).start()
-
-    give_half(zed)
-
-    def send_near(step, _):
+    def send_other(step, _):
         group = order(step)
 
-        @pl.when(step > 0)
-        def _():
-            regroup(0, group)
-
-        send_row(0, group)
-
-        @pl.when(jnp.logical_or(group == my_g, group == partner_g))
+        @pl.when(jnp.logical_and(lax.rem(group, 2) != core, group != partner_g))
+        def _():
+            send_row(0, group)
+
+        @pl.when(group == partner_g)
         def _():
             send_rest(0, group)
 
         return 0
 
-    lax.fori_loop(0, groups, send_near, 0)
-
+    lax.fori_loop(0, groups, send_other, 0)
     pl.semaphore_wait(plane_sem, 3)
 
     def send_far(step, _):
@@ -312,9 +340,10 @@
 
     lax.fori_loop(0, lst_n, align_weights, 0)
 
+    def arrived(tile):
+        total_wait(recv_in.at[tile], in_recv.at[tile])
+
     def bin_tile(tile):
-        total_wait(recv_in.at[tile], in_recv.at[tile])
-
         def widen(src, _):
             at = pl.ds(pl.multiple_of(src * block, block), block)
             for n in range(nights):
@@ -358,43 +387,51 @@
             return 0
 
         lax.fori_loop(0, bl_n, apply_filter, 0)
-        for tile in range(first, last):
-
-            def send_back(i, _):
-                q = lax.rem(me + i, lst_n)
-                pltpu.make_async_remote_copy(
-                    send_out.at[tile, q],
-                    recv_out.at[tile, me],
-                    out_send.at[tile],
-                    out_recv.at[tile],
-                    device_id={"lst": q},
-                ).start()
-                return 0
-
-            lax.fori_loop(1, lst_n, send_back, 0)
-            pltpu.make_async_copy(
-                send_out.at[tile, me], recv_out.at[tile, me], out_recv.at[tile]
-            ).start()
+
+    def send_back(tile):
+        for db, dx in FAR_TO_NEAR:
+            for dc in (0, 1):
+                b = lax.rem(my_b + db, bls)
+                group = lax.rem(jnp.where(dc == 1, partner_g, my_g) + 2 * dx, groups)
+                send_result(tile, b * groups + group)
+        send_result(tile, partner)
+        pltpu.make_async_copy(
+            send_out.at[tile, me], recv_out.at[tile, me], out_recv.at[tile]
+        ).start()
+
+    def send_result(tile, q):
+        pltpu.make_async_remote_copy(
+            send_out.at[tile, q],
+            recv_out.at[tile, me],
+            out_send.at[tile],
+            out_recv.at[tile],
+            device_id={"lst": q},
+        ).start()
 
     for tile in range(tiles - 1):
+        arrived(tile)
         bin_tile(tile)
     total_wait(filt.at[:, 1 - core], f_swap.at[1])
     filter_tiles(0, tiles - 1)
+    for tile in range(tiles - 1):
+        send_back(tile)
+    arrived(tiles - 1)
     bin_tile(tiles - 1)
     filter_tiles(tiles - 1, tiles)
+    send_back(tiles - 1)
 
     def place_tile(tile, _):
         total_wait(recv_out.at[tile], out_recv.at[tile])
 
         def place(group, _):
             lanes = pl.ds(pl.multiple_of((tile * groups + group) * LANES, LANES), LANES)
-            for which, out in ((0, out_f), (1, out_s)):
+            for which in range(2):
                 for b in range(bls):
                     stage[which, pl.ds(b, block, stride=bls), :] = recv_out[
                         tile, b * groups + group, which
                     ].astype(jnp.float32)
                 for t in range(block):
-                    out[t, :, lanes] = stage[which, t * bls : (t + 1) * bls, :].astype(
+                    out[which, t, :, lanes] = stage[which, t * bls : (t + 1) * bls, :].astype(
                         jnp.bfloat16
                     )
             return 0
@@ -424,15 +461,15 @@
     tiles = width // (groups * LANES)
     sizes = (nights, block, bls, lst_n, bl_n, tiles)
     bf16, f32 = jnp.bfloat16, jnp.float32
-    out = jax.ShapeDtypeStruct((block, bls, width), bf16)
+    out = jax.ShapeDtypeStruct((2, block, bls, width), bf16)
     vmem = pl.BlockSpec(memory_space=pltpu.VMEM)
     hbm = pl.BlockSpec(memory_space=pltpu.HBM)
     dma = pltpu.SemaphoreType.DMA
-    return pl.pallas_call(
+    both = pl.pallas_call(
         functools.partial(kernel, sizes),
-        out_shape=(out, out),
+        out_shape=out,
         in_specs=[hbm] * 5,
-        out_specs=(vmem, vmem),
+        out_specs=vmem,
         scratch_shapes=[
             pltpu.SMEM((nights,), jnp.int32),
             pltpu.SMEM((nights,), jnp.int32),
@@ -453,6 +490,7 @@
             pltpu.VMEM((tiles, lst_n, 2, block, LANES), bf16),
             pltpu.VMEM((tiles, lst_n, 2, block, LANES), bf16),
             pltpu.SemaphoreType.REGULAR,
+            pltpu.SemaphoreType.REGULAR,
             dma((tiles,)),
             dma((3,)),
             dma((tiles,)),
@@ -468,7 +506,7 @@
             dma((tiles,)),
         ],
         compiler_params=pltpu.CompilerParams(
-            collective_id=0, has_side_effects=True, vmem_limit_bytes=48 * 2**20
+            collective_id=0, has_side_effects=True, vmem_limit_bytes=40 * 2**20
         ),
         cost_estimate=pl.CostEstimate(
             flops=2 * bins * bins * tiles * LANES, bytes_accessed=8 * 2**20, transcendentals=0
@@ -485,6 +523,7 @@
             )
         ]
     )
+    return both[0], both[1]
 
 
 def solution(mesh):

time: 62.7 us -> 62.4 us (level)
    unnamed x2 -> x0, local copies, waits for them, and re-layouts: 1.76 us -> none
    squeeze x0 -> x1, local copies, waits for them, and re-layouts: none -> 1.68 us  [shards(): return (both[0], both[1])]
where the time goes in v4:
time: 62.4 us; the launch traced here: 62.3 us
  Pallas kernels  60 us (96%)
  local copies, waits for them, and re-layouts  1.68 us (3%)
  between operations  0.64 us (1%)
    pallas_call x1, Pallas kernels, shards(): pl.pallas_call(functools.partial(kernel, sizes), out_shape=out, in_specs=...  60 us
    squeeze x1, local copies, waits for them, and re-layouts, shards(): return (both[0], both[1])  1.68 us

profile of v4, /device:TPU:1, one launch (start us, length us, event | category | flops | bytes accessed | tf_op | source)
XLA Modules:
  0.0 62.3 jit_solution(3124049429121890288)
XLA Ops:
  0.6 60.0 %shard_map.68 = bf16[2,32,4,3072]{3,2,1,0:T(4,128)(2,1)S(1)} custom-call(s32[4]{0:T(128)} %start_hbm.1, s32[4]{0:T(128)} %cover_hbm.1, s32[4,4,32]{2,1,0:T(4,128)} %bitcast.5, bf16[4,32,4,3072]{3,2,1,0:T(4,128)(2,1)} %vis_hbm.1, bf16[128,1024]{1,0:T(8,128)(2,1)} %filt_hbm.1), custom_call_target="tpu_custom_call" | custom-call | flops 805306368 | bytes 8388608 | tf_op jit(solution)/shard_map/pallas_call | solution.py:468
  60.6 1.7 %slice_bitcast_fusion = (bf16[32,4,3072]{2,1,0:T(4,128)(2,1)}, bf16[32,4,3072]{2,1,0:T(4,128)(2,1)}) fusion(bf16[2,32,4,3072]{3,2,1,0:T(4,128)(2,1)S(1)} %shard_map.68), kind=kLoop, calls=%fused_computation | loop fusion | bytes 3145728 | tf_op jit(solution)/shard_map/squeeze | solution.py:526

commit v5 on v4

--- a/solution.py
+++ b/solution.py
@@ -87,6 +87,7 @@
         for tile in range(tiles)
     ]
 
+    loads[0].start()
     barrier = pltpu.get_barrier_semaphore()
     greeted = 7
     for i in (2, 1, 3):
@@ -104,7 +105,6 @@
             lambda: pl.semaphore_signal(barrier, 1, device_id={"bl": bl_n - 1})
         )
 
-    loads[0].start()
     for copy in small:
         copy.start()
     own_half = pltpu.make_async_copy(
@@ -423,20 +423,20 @@
     def place_tile(tile, _):
         total_wait(recv_out.at[tile], out_recv.at[tile])
 
-        def place(group, _):
-            lanes = pl.ds(pl.multiple_of((tile * groups + group) * LANES, LANES), LANES)
+        def place(pair, _):
             for which in range(2):
-                for b in range(bls):
-                    stage[which, pl.ds(b, block, stride=bls), :] = recv_out[
-                        tile, b * groups + group, which
-                    ].astype(jnp.float32)
+                for i in range(2):
+                    for b in range(bls):
+                        stage[which, pl.ds(i * bls + b, block, stride=2 * bls), :] = recv_out[
+                            tile, b * groups + 2 * pair + i, which
+                        ].astype(jnp.float32)
                 for t in range(block):
-                    out[which, t, :, lanes] = stage[which, t * bls : (t + 1) * bls, :].astype(
-                        jnp.bfloat16
-                    )
+                    out[which, t, tile * (groups // 2) + pair] = stage[
+                        which, t * 2 * bls : (t + 1) * 2 * bls, :
+                    ].astype(jnp.bfloat16)
             return 0
 
-        lax.fori_loop(0, groups, place, 0)
+        lax.fori_loop(0, groups // 2, place, 0)
         return 0
 
     lax.fori_loop(0, tiles, place_tile, 0)
@@ -461,7 +461,7 @@
     tiles = width // (groups * LANES)
     sizes = (nights, block, bls, lst_n, bl_n, tiles)
     bf16, f32 = jnp.bfloat16, jnp.float32
-    out = jax.ShapeDtypeStruct((2, block, bls, width), bf16)
+    out = jax.ShapeDtypeStruct((2, block, tiles * groups // 2, 2 * bls, LANES), bf16)
     vmem = pl.BlockSpec(memory_space=pltpu.VMEM)
     hbm = pl.BlockSpec(memory_space=pltpu.HBM)
     dma = pltpu.SemaphoreType.DMA
@@ -475,7 +475,7 @@
             pltpu.SMEM((nights,), jnp.int32),
             pltpu.VMEM((nights, bls, block), jnp.int32),
             pltpu.VMEM((tiles, nights, block, bls, groups * LANES), bf16),
-            pltpu.VMEM((nights, block * bls, LANES), f32),
+            pltpu.VMEM((nights, 2 * block * bls, LANES), f32),
             pltpu.VMEM((tiles, lst_n, nights, block, LANES), bf16),
             pltpu.VMEM((tiles, lst_n, nights, block, LANES), bf16),
             pltpu.VMEM((bls, 1, nights * block), f32),
@@ -523,7 +523,12 @@
             )
         ]
     )
-    return both[0], both[1]
+
+    def unfold(x):
+        x = x.reshape(block, tiles * groups, bls, LANES)
+        return jnp.swapaxes(x, 1, 2).reshape(block, bls, width)
+
+    return unfold(both[0]), unfold(both[1])
 
 
 def solution(mesh):

time: 62.4 us -> 61.8 us (level)
    squeeze x1 -> x0, local copies, waits for them, and re-layouts: 1.68 us -> none  [shards(): return (both[0], both[1])]
    slice x0 -> x1, local copies, waits for them, and re-layouts: none -> 1.24 us  [shards(): return (unfold(both[0]), unfold(both[1]))]
where the time goes in v5:
time: 61.8 us; the launch traced here: 61.7 us
  Pallas kernels  59.9 us (97%)
  local copies, waits for them, and re-layouts  1.24 us (2%)
  between operations  0.64 us (1%)
    pallas_call x1, Pallas kernels, shards(): pl.pallas_call(functools.partial(kernel, sizes), out_shape=out, in_specs=...  59.9 us
    slice x1, local copies, waits for them, and re-layouts, shards(): return (unfold(both[0]), unfold(both[1]))  1.24 us

profile of v5, /device:TPU:1, one launch (start us, length us, event | category | flops | bytes accessed | tf_op | source)
XLA Modules:
  0.0 61.7 jit_solution(11139124529380807546)
XLA Ops:
  0.6 59.9 %shard_map.68 = bf16[2,32,12,8,128]{4,3,2,1,0:T(8,128)(2,1)S(1)} custom-call(s32[4]{0:T(128)} %start_hbm.1, s32[4]{0:T(128)} %cover_hbm.1, s32[4,4,32]{2,1,0:T(4,128)} %bitcast.13, bf16[4,32,4,3072]{3,2,1,0:T(4,128)(2,1)} %vis_hbm.1, bf16[128,1024]{1,0:T(8,128)(2,1)} %filt_hbm.1), custom_call_target="tpu_custom_call" | custom-call | flops 805306368 | bytes 8388608 | tf_op jit(solution)/shard_map/pallas_call | solution.py:468
  60.5 1.2 %fusion = (bf16[1,32,12,8,128]{4,3,2,1,0:T(8,128)(2,1)}, bf16[1,32,12,8,128]{4,3,2,1,0:T(8,128)(2,1)}) fusion(bf16[2,32,12,8,128]{4,3,2,1,0:T(8,128)(2,1)S(1)} %shard_map.68), kind=kLoop, calls=%fused_computation | loop fusion | bytes 3145728 | tf_op jit(solution)/shard_map/slice | solution.py:531

commit v6 on v5

--- a/solution.py
+++ b/solution.py
@@ -111,8 +111,6 @@
         filt_hbm.at[pl.ds(pl.multiple_of(core * half, half), half)], filt.at[zed, core], f_own
     )
     own_half.start()
-    for load in loads[1:]:
-        load.start()
 
     def regroup(tile, group):
         lanes = pl.ds(pl.multiple_of(group * LANES, LANES), LANES)
@@ -199,6 +197,8 @@
             give_half(below)
 
     loads[0].wait()
+    for load in loads[1:]:
+        load.start()
     regroup(0, order(0))
     own_half.wait()
     if bl_n > 1:
@@ -423,20 +423,23 @@
     def place_tile(tile, _):
         total_wait(recv_out.at[tile], out_recv.at[tile])
 
-        def place(pair, _):
-            for which in range(2):
+        def place(half_of_pairs, _):
+            for slot in range(4):
+                pair, which = 2 * half_of_pairs + slot // 2, slot % 2
                 for i in range(2):
                     for b in range(bls):
-                        stage[which, pl.ds(i * bls + b, block, stride=2 * bls), :] = recv_out[
+                        stage[slot, pl.ds(i * bls + b, block, stride=2 * bls), :] = recv_out[
                             tile, b * groups + 2 * pair + i, which
                         ].astype(jnp.float32)
+            for slot in range(4):
+                pair, which = 2 * half_of_pairs + slot // 2, slot % 2
                 for t in range(block):
                     out[which, t, tile * (groups // 2) + pair] = stage[
-                        which, t * 2 * bls : (t + 1) * 2 * bls, :
+                        slot, t * 2 * bls : (t + 1) * 2 * bls, :
                     ].astype(jnp.bfloat16)
             return 0
 
-        lax.fori_loop(0, groups // 2, place, 0)
+        lax.fori_loop(0, groups // 4, place, 0)
         return 0
 
     lax.fori_loop(0, tiles, place_tile, 0)

time: 61.8 us -> 61.8 us (level)
  no operation moved by 1% of the time
where the time goes in v6:
time: 61.8 us; the launch traced here: 61.7 us
  Pallas kernels  59.8 us (97%)
  local copies, waits for them, and re-layouts  1.24 us (2%)
  between operations  0.64 us (1%)
    pallas_call x1, Pallas kernels, shards(): pl.pallas_call(functools.partial(kernel, sizes), out_shape=out, in_specs=...  59.8 us
    slice x1, local copies, waits for them, and re-layouts, shards(): return (unfold(both[0]), unfold(both[1]))  1.24 us

profile of v6, /device:TPU:1, one launch (start us, length us, event | category | flops | bytes accessed | tf_op | source)
XLA Modules:
  0.0 61.7 jit_solution(17322783252084021621)
XLA Ops:
  0.6 59.8 %shard_map.68 = bf16[2,32,12,8,128]{4,3,2,1,0:T(8,128)(2,1)S(1)} custom-call(s32[4]{0:T(128)} %start_hbm.1, s32[4]{0:T(128)} %cover_hbm.1, s32[4,4,32]{2,1,0:T(4,128)} %bitcast.13, bf16[4,32,4,3072]{3,2,1,0:T(4,128)(2,1)} %vis_hbm.1, bf16[128,1024]{1,0:T(8,128)(2,1)} %filt_hbm.1), custom_call_target="tpu_custom_call" | custom-call | flops 805306368 | bytes 8388608 | tf_op jit(solution)/shard_map/pallas_call | solution.py:471
  60.5 1.2 %fusion = (bf16[1,32,12,8,128]{4,3,2,1,0:T(8,128)(2,1)}, bf16[1,32,12,8,128]{4,3,2,1,0:T(8,128)(2,1)}) fusion(bf16[2,32,12,8,128]{4,3,2,1,0:T(8,128)(2,1)S(1)} %shard_map.68), kind=kLoop, calls=%fused_computation | loop fusion | bytes 3145728 | tf_op jit(solution)/shard_map/slice | solution.py:534
